TPU v7x, 128 devices: a whole 4x4x4 slice. The times are simulated.
128 devices in a mesh: rep: 2 (over x_hi), ctx: 32 (over z, x_lo, y), head: 2 (over core).
Axes of the slice: x: 4 (x_hi: 2, x_lo: 2; x = x_hi * 2 + x_lo), y: 4, z: 4, core: 2. Of those that a mesh axis runs over, the one named last changes fastest.
Arguments:
- tokens: bfloat16 [2, 6144, 1024], P('rep', 'ctx'), may hold values from -6 to 6
- segments: int32 [2, 6144], P('rep', 'ctx'), may hold values from 0 to 2, as said below
- positions: int32 [2, 6144], P('rep', 'ctx'), may hold values from 0 to 5951, as said below
- cotangent: bfloat16 [2, 6144, 1024], P('rep', 'ctx'), may hold values from -6 to 6
- query_weight: bfloat16 [1024, 2048], P('ctx', 'head'), may hold values from -0.1875 to 0.1875
- key_weight: bfloat16 [1024, 1024], P('ctx', 'head'), may hold values from -0.1875 to 0.1875
- value_weight: bfloat16 [1024, 1024], P('ctx', 'head'), may hold values from -0.1875 to 0.1875
- out_weight: bfloat16 [2048, 1024], P('head', 'ctx'), may hold values from -4 to 4
- attn_gain: bfloat16 [1024], P('ctx'), may hold values from 0.5 to 1.5
- query_gain: bfloat16 [128], replicated, may hold values from 0.5 to 1.5
- key_gain: bfloat16 [128], replicated, may hold values from 0.5 to 1.5
- gate_weight: bfloat16 [1024, 3072], P('ctx', 'head'), may hold values from -0.1875 to 0.1875
- up_weight: bfloat16 [1024, 3072], P('ctx', 'head'), may hold values from -0.1875 to 0.1875
- down_weight: bfloat16 [3072, 1024], P('head', 'ctx'), may hold values from -0.109375 to 0.109375
- mlp_gain: bfloat16 [1024], P('ctx'), may hold values from 0.5 to 1.5
Outputs:
- result: bfloat16 [2, 6144, 1024], P('rep', 'ctx')
- input_grad: bfloat16 [2, 6144, 1024], P('rep', 'ctx')
- grad_query_weight: float32 [1024, 2048], P('ctx', 'head')
- grad_key_weight: float32 [1024, 1024], P('ctx', 'head')
- grad_value_weight: float32 [1024, 1024], P('ctx', 'head')
- grad_out_weight: float32 [2048, 1024], P('head', 'ctx')
- grad_attn_gain: float32 [1024], P('ctx')
- grad_query_gain: float32 [128], replicated
- grad_key_gain: float32 [128], replicated
- grad_gate_weight: float32 [1024, 3072], P('ctx', 'head')
- grad_up_weight: float32 [1024, 3072], P('ctx', 'head')
- grad_down_weight: float32 [3072, 1024], P('head', 'ctx')
- grad_mlp_gain: float32 [1024], P('ctx')
Inputs may be any that keep to these rules, and one draw needn't show every extreme that they name: `segments`: segment numbers never fall along a sequence. Document 0 holds the first tokens, 1 to 191 of them; document 1 follows with exactly 5952 tokens; document 2 holds the rest, at least one token. `positions`: each token's position within its document: 0 at a document's first token, rising by one per token.
All inputs are finite; a program needn't handle non-finite values.
Results may differ from a plain program's by a relative error of at most 0.03.
Values may be sent and summed in bfloat16 or wider, within the bound.
A program may use at most 192 MiB of HBM per device.

v0:
```python
import functools
import math

import jax
import jax.numpy as jnp
from jax import lax
from jax.sharding import Mesh
from jax.sharding import PartitionSpec as P

HEAD_DIM = 128
CTX = ("ctx_0", "ctx_1", "ctx_2")
REP_CTX_HEAD = ("rep", "ctx_0", "ctx_1", "ctx_2", "head")


EPSILON = 1e-06
ROPE_BASE = 1000000.0
MASKED_SCORE = -1e30


def gather_turned(arrays, axis, dims):
    turned = [jnp.moveaxis(a, dim, 0) for a, dim in zip(arrays, dims)]
    both = jnp.concatenate([t.reshape(len(t), -1) for t in turned], axis=1)
    result, at, done = (lax.all_gather(both, axis, axis=0, tiled=True), 0, [])
    for t, dim in zip(turned, dims):
        section = result[:, at : at + t[0].size].reshape(-1, *t.shape[1:])
        done.append(jnp.moveaxis(section, 0, dim))
        at += t[0].size
    return tuple(done)


def side_by_side(arrays, axis, dim, along):
    widths = [math.prod(a.shape[along:]) for a in arrays]
    both = jnp.concatenate(
        [a.reshape(*a.shape[:along], w) for a, w in zip(arrays, widths)], axis=along
    )
    result = lax.all_gather(both, axis, axis=dim, tiled=True)
    tiles = jnp.split(result, [sum(widths[:k]) for k in range(1, len(widths))], axis=along)
    return tuple(
        (b.reshape(*result.shape[:along], *a.shape[along:]) for a, b in zip(arrays, tiles))
    )


def sent_to_all(x, axis):
    peers = lax.axis_size(axis)
    return lax.all_to_all(jnp.broadcast_to(x[None], (peers, *x.shape)), axis, 0, 0, tiled=True)


def of_everyone(x, axis):
    return sent_to_all(x, axis).astype(jnp.float32).sum(axis=0)


def side_by_side_2(arrays, axis, dim, along):
    ends, at = ([], 0)
    for a in arrays[:-1]:
        at += a.shape[along]
        ends.append(at)
    both = jnp.concatenate(arrays, axis=along)
    return tuple(
        jnp.split(lax.psum_scatter(both, axis, scatter_dimension=dim, tiled=True), ends, axis=along)
    )


def side_by_side_3(arrays, axis, dim, along):
    columns = [a.reshape(*a.shape[:along], -1) for a in arrays]
    both = jnp.concatenate(columns, axis=along)
    result, at, done = (lax.psum_scatter(both, axis, scatter_dimension=dim, tiled=True), 0, [])
    for a, column in zip(arrays, columns):
        section = result[..., at : at + column.shape[along]]
        done.append(section.reshape(*section.shape[:along], *a.shape[along:]))
        at += column.shape[along]
    return tuple(done)


def one_axis_at_a_time(x, axes):
    return functools.reduce(lax.psum, axes, x)


def rms_scale(values, gain):
    return values * lax.rsqrt(jnp.mean(values * values, axis=-1, keepdims=True) + EPSILON) * gain


def rotate(values, places):
    half_dim = values.shape[-1] // 2
    inverse = ROPE_BASE ** (-jnp.arange(half_dim, dtype=jnp.float32) / half_dim)
    angles = places.astype(jnp.float32)[:, None] * inverse[None, :]
    cosine = jnp.cos(angles)[:, None, :]
    sine_part = jnp.sin(angles)[:, None, :]
    first_half = values[..., :half_dim]
    second_half = values[..., half_dim:]
    return jnp.concatenate(
        [
            first_half * cosine - second_half * sine_part,
            second_half * cosine + first_half * sine_part,
        ],
        axis=-1,
    )


def dense(left, right):
    return jnp.dot(left, right, preferred_element_type=jnp.float32)


def dense_left(left, right):
    return lax.dot_general(
        left, right, (((0,), (0,)), ((), ())), preferred_element_type=jnp.float32
    )


def dense_right(left, right):
    return lax.dot_general(
        left, right, (((1,), (1,)), ((), ())), preferred_element_type=jnp.float32
    )


def split_keys(key_rows, value_rows, key_docs, first_key, head_size):
    key_count = key_rows.shape[0]
    block_size = math.gcd(key_count, 512)
    block_count = key_count // block_size
    key_groups = key_rows.shape[1] // head_size
    key_split = key_rows.reshape(block_count, block_size, key_groups, head_size)
    value_split = value_rows.reshape(block_count, block_size, key_groups, head_size)
    doc_split = key_docs.reshape(block_count, block_size)
    block_firsts = first_key + jnp.arange(block_count, dtype=jnp.int32) * block_size
    return ((key_split, value_split, doc_split, block_firsts), block_size)


def key_blocks(
    carried_state, key_rows, value_rows, key_docs, first_key, query_heads, query_docs, query_index
):
    head_size = query_heads.shape[3]
    factor = 1.0 / math.sqrt(head_size)
    blocks, block_size = split_keys(key_rows, value_rows, key_docs, first_key, head_size)

    def visit_block(running_state, block_entry):
        running_top, running_total, running_sum = running_state
        key_block, value_block, doc_block, block_first = block_entry
        scores = (
            jnp.einsum("qgrd,kgd->grqk", query_heads, key_block, preferred_element_type=jnp.float32)
            * factor
        )
        key_index = block_first + jnp.arange(block_size, dtype=jnp.int32)
        allowed = (key_index[None, :] <= query_index[:, None]) & (
            doc_block[None, :] == query_docs[:, None]
        )
        scores = jnp.where(allowed, scores, MASKED_SCORE)
        new_top = jnp.maximum(running_top, jnp.max(scores, axis=-1))
        weights = jnp.where(allowed, jnp.exp(scores - new_top[..., None]), 0.0)
        shrink = jnp.exp(running_top - new_top)
        running_total = running_total * shrink + jnp.sum(weights, axis=-1)
        running_sum = running_sum * shrink[..., None] + jnp.einsum(
            "grqk,kgd->grqd",
            weights.astype(jnp.bfloat16),
            value_block,
            preferred_element_type=jnp.float32,
        )
        return ((new_top, running_total, running_sum), None)

    final_state, ignored = lax.scan(visit_block, carried_state, blocks)
    return final_state


def key_gradients(
    query_heads,
    grad_heads,
    log_total,
    delta_rows,
    query_docs,
    query_index,
    key_rows,
    value_rows,
    key_docs,
):
    head_size = query_heads.shape[3]
    factor = 1.0 / math.sqrt(head_size)
    key_count = key_rows.shape[0]
    blocks, block_size = split_keys(key_rows, value_rows, key_docs, 0, head_size)

    def visit_block(grad_query, block_entry):
        key_block, value_block, doc_block, block_first = block_entry
        scores = (
            jnp.einsum("qgrd,kgd->grqk", query_heads, key_block, preferred_element_type=jnp.float32)
            * factor
        )
        key_index = block_first + jnp.arange(block_size, dtype=jnp.int32)
        allowed = (key_index[None, :] <= query_index[:, None]) & (
            doc_block[None, :] == query_docs[:, None]
        )
        probs = jnp.where(
            allowed, jnp.exp(jnp.where(allowed, scores, MASKED_SCORE) - log_total[..., None]), 0.0
        )
        grad_value = jnp.einsum(
            "grqk,qgrd->kgd",
            probs.astype(jnp.bfloat16),
            grad_heads,
            preferred_element_type=jnp.float32,
        )
        grad_probs = jnp.einsum(
            "qgrd,kgd->grqk", grad_heads, value_block, preferred_element_type=jnp.float32
        )
        grad_scores = (probs * (grad_probs - delta_rows[..., None])).astype(jnp.bfloat16)
        grad_query = grad_query + jnp.einsum(
            "grqk,kgd->qgrd", grad_scores, key_block, preferred_element_type=jnp.float32
        )
        grad_key = (
            jnp.einsum(
                "grqk,qgrd->kgd", grad_scores, query_heads, preferred_element_type=jnp.float32
            )
            * factor
        )
        return (grad_query, (grad_key, grad_value))

    start_grad = jnp.zeros(query_heads.shape, jnp.float32)
    grad_query, (key_parts, value_parts) = lax.scan(visit_block, start_grad, blocks)
    return (
        grad_query * factor,
        key_parts.reshape(key_count, -1),
        value_parts.reshape(key_count, -1),
    )


def on_device(
    tokens,
    segments,
    positions,
    cotangent,
    query_weight,
    key_weight,
    value_weight,
    out_weight,
    attn_gain,
    query_gain,
    key_gain,
    gate_weight,
    up_weight,
    down_weight,
    mlp_gain,
):
    inputs = tokens[0].astype(jnp.float32)
    query_docs = segments[0].astype(jnp.bfloat16)
    places = positions[0]
    row_count = inputs.shape[0]
    query_index = lax.axis_index(CTX) * row_count + jnp.arange(row_count, dtype=jnp.int32)
    (
        full_query,
        full_key,
        full_value,
        full_out,
        gain_one,
        full_gate,
        full_up,
        full_down,
        gain_two,
    ) = gather_turned(
        (
            query_weight,
            key_weight,
            value_weight,
            out_weight,
            attn_gain,
            gate_weight,
            up_weight,
            down_weight,
            mlp_gain,
        ),
        CTX,
        (0, 0, 0, 1, 0, 0, 0, 1, 0),
    )
    gain_one_wide = gain_one.astype(jnp.float32)
    gain_two_wide = gain_two.astype(jnp.float32)
    normed_low = rms_scale(inputs, gain_one_wide).astype(jnp.bfloat16)
    query_pre = dense(normed_low, full_query)
    key_pre = dense(normed_low, full_key)
    value_low = dense(normed_low, full_value).astype(jnp.bfloat16)
    head_count = query_pre.shape[1] // HEAD_DIM
    key_groups = key_pre.shape[1] // HEAD_DIM
    group_size = head_count // key_groups

    def shape_heads(query_in, key_in, query_scale, key_scale):
        query_out = rotate(
            rms_scale(query_in.reshape(row_count, head_count, HEAD_DIM), query_scale), places
        )
        key_out = rotate(
            rms_scale(key_in.reshape(row_count, key_groups, HEAD_DIM), key_scale), places
        )
        return (query_out, key_out)

    (query_rot, key_rot), heads_pull = jax.vjp(
        shape_heads,
        query_pre,
        key_pre,
        query_gain.astype(jnp.float32),
        key_gain.astype(jnp.float32),
    )
    query_heads = query_rot.astype(jnp.bfloat16).reshape(
        row_count, key_groups, group_size, HEAD_DIM
    )
    key_low = key_rot.astype(jnp.bfloat16).reshape(row_count, key_groups * HEAD_DIM)
    start_state = (
        jnp.full((key_groups, group_size, row_count), MASKED_SCORE, jnp.float32),
        jnp.zeros((key_groups, group_size, row_count), jnp.float32),
        jnp.zeros((key_groups, group_size, row_count, HEAD_DIM), jnp.float32),
    )
    piece = side_by_side((key_low, value_low, query_docs), CTX, 0, 1)
    running_top, running_total, running_sum = key_blocks(
        start_state,
        piece[0],
        piece[1],
        piece[2],
        jnp.int32(0),
        query_heads,
        query_docs,
        query_index,
    )
    out_heads = running_sum / running_total[..., None]
    log_total = running_top + jnp.log(running_total)
    attended_low = (
        jnp.transpose(out_heads, (2, 0, 1, 3))
        .reshape(row_count, head_count * HEAD_DIM)
        .astype(jnp.bfloat16)
    )
    hidden_in = inputs + of_everyone(
        dense(attended_low, full_out).astype(jnp.bfloat16), "head"
    ).astype(jnp.float32)
    normed_two_low = rms_scale(hidden_in, gain_two_wide).astype(jnp.bfloat16)
    gate_pre = dense(normed_two_low, full_gate)
    up_pre = dense(normed_two_low, full_up)

    def swiglu(gate_in, up_in):
        return jax.nn.silu(gate_in) * up_in

    activated, swiglu_pull = jax.vjp(swiglu, gate_pre, up_pre)
    activated_low = activated.astype(jnp.bfloat16)
    mlp_out = of_everyone(dense(activated_low, full_down).astype(jnp.bfloat16), "head").astype(
        jnp.float32
    )
    result = (hidden_in + mlp_out).astype(jnp.bfloat16)
    (
        full_query,
        full_key,
        full_value,
        full_out,
        gain_one,
        full_gate,
        full_up,
        full_down,
        gain_two,
    ) = gather_turned(
        (
            query_weight,
            key_weight,
            value_weight,
            out_weight,
            attn_gain,
            gate_weight,
            up_weight,
            down_weight,
            mlp_gain,
        ),
        CTX,
        (0, 0, 0, 1, 0, 0, 0, 1, 0),
    )
    gain_one_wide = gain_one.astype(jnp.float32)
    gain_two_wide = gain_two.astype(jnp.float32)
    grad_result = cotangent[0]
    grad_down = dense_left(activated_low, grad_result)
    grad_activated = dense_right(grad_result, full_down)
    grad_gate_wide, grad_up_wide = swiglu_pull(grad_activated)
    grad_gate_low = grad_gate_wide.astype(jnp.bfloat16)
    grad_up_low = grad_up_wide.astype(jnp.bfloat16)
    grad_gate = dense_left(normed_two_low, grad_gate_low)
    grad_up = dense_left(normed_two_low, grad_up_low)
    grad_normed_two = of_everyone(
        (dense_right(grad_gate_low, full_gate) + dense_right(grad_up_low, full_up)).astype(
            jnp.bfloat16
        ),
        "head",
    ).astype(jnp.float32)
    ignored_two, norm_two_pull = jax.vjp(rms_scale, hidden_in, gain_two_wide)
    grad_hidden_part, grad_gain_two = norm_two_pull(grad_normed_two)
    grad_hidden = grad_result.astype(jnp.float32) + grad_hidden_part
    grad_hidden_low = grad_hidden.astype(jnp.bfloat16)
    grad_out = dense_left(attended_low, grad_hidden_low)
    grad_heads = (
        dense_right(grad_hidden_low, full_out)
        .astype(jnp.bfloat16)
        .reshape(row_count, key_groups, group_size, HEAD_DIM)
    )
    delta_rows = jnp.einsum("qgrd,grqd->grq", grad_heads.astype(jnp.float32), out_heads)
    back_keys, back_values, back_docs = side_by_side((key_low, value_low, query_docs), CTX, 0, 1)
    grad_query_heads, key_terms, value_terms = key_gradients(
        query_heads,
        grad_heads,
        log_total,
        delta_rows,
        query_docs,
        query_index,
        back_keys,
        back_values,
        back_docs,
    )
    grad_keys, grad_values = tuple(
        (
            part.astype(jnp.float32)
            for part in side_by_side_2(
                (key_terms.astype(jnp.bfloat16), value_terms.astype(jnp.bfloat16)), CTX, 0, 1
            )
        )
    )
    grad_query_pre, grad_key_pre, grad_query_gain, grad_key_gain = heads_pull(
        (
            grad_query_heads.reshape(row_count, head_count, HEAD_DIM),
            grad_keys.reshape(row_count, key_groups, HEAD_DIM),
        )
    )
    query_grad_low = grad_query_pre.astype(jnp.bfloat16)
    key_grad_low = grad_key_pre.astype(jnp.bfloat16)
    value_grad_low = grad_values.astype(jnp.bfloat16)
    grad_wquery = dense_left(normed_low, query_grad_low)
    grad_wkey = dense_left(normed_low, key_grad_low)
    grad_wvalue = dense_left(normed_low, value_grad_low)
    grad_normed = of_everyone(
        (
            dense_right(query_grad_low, full_query)
            + dense_right(key_grad_low, full_key)
            + dense_right(value_grad_low, full_value)
        ).astype(jnp.bfloat16),
        "head",
    ).astype(jnp.float32)
    ignored_one, norm_one_pull = jax.vjp(rms_scale, inputs, gain_one_wide)
    grad_input_part, grad_gain_one = norm_one_pull(grad_normed)
    input_grad = (grad_hidden + grad_input_part).astype(jnp.bfloat16)
    (
        own_query,
        own_key,
        own_value,
        own_out,
        own_gain_one,
        own_gate,
        own_up,
        own_down,
        own_gain_two,
    ) = (
        *tuple(
            (
                part.astype(jnp.float32)
                for part in side_by_side_2(
                    (
                        grad_wquery.astype(jnp.bfloat16),
                        grad_wkey.astype(jnp.bfloat16),
                        grad_wvalue.astype(jnp.bfloat16),
                    ),
                    CTX,
                    0,
                    1,
                )
            )
        ),
        lax.psum_scatter(
            grad_out.astype(jnp.bfloat16), CTX, scatter_dimension=1, tiled=True
        ).astype(jnp.float32),
        *tuple(
            (
                part.astype(jnp.float32)
                for part in side_by_side_3(
                    (
                        grad_gain_one.astype(jnp.bfloat16),
                        grad_gate.astype(jnp.bfloat16),
                        grad_up.astype(jnp.bfloat16),
                    ),
                    CTX,
                    0,
                    1,
                )
            )
        ),
        lax.psum_scatter(
            grad_down.astype(jnp.bfloat16), CTX, scatter_dimension=1, tiled=True
        ).astype(jnp.float32),
        lax.psum_scatter(
            grad_gain_two.astype(jnp.bfloat16), CTX, scatter_dimension=0, tiled=True
        ).astype(jnp.float32),
    )
    (
        sum_query,
        sum_key,
        sum_value,
        sum_out,
        sum_gain_one,
        sum_gate,
        sum_up,
        sum_down,
        sum_gain_two,
    ) = (
        of_everyone(own_query.astype(jnp.bfloat16), "rep").astype(jnp.float32),
        of_everyone(own_key.astype(jnp.bfloat16), "rep").astype(jnp.float32),
        of_everyone(own_value.astype(jnp.bfloat16), "rep").astype(jnp.float32),
        of_everyone(own_out.astype(jnp.bfloat16), "rep").astype(jnp.float32),
        of_everyone(own_gain_one.astype(jnp.bfloat16), "rep").astype(jnp.float32),
        of_everyone(own_gate.astype(jnp.bfloat16), "rep").astype(jnp.float32),
        of_everyone(own_up.astype(jnp.bfloat16), "rep").astype(jnp.float32),
        of_everyone(own_down.astype(jnp.bfloat16), "rep").astype(jnp.float32),
        of_everyone(own_gain_two.astype(jnp.bfloat16), "rep").astype(jnp.float32),
    )
    total_query_gain, total_key_gain = (
        one_axis_at_a_time(grad_query_gain, REP_CTX_HEAD),
        one_axis_at_a_time(grad_key_gain, REP_CTX_HEAD),
    )
    return (
        result[None],
        input_grad[None],
        sum_query,
        sum_key,
        sum_value,
        sum_out,
        sum_gain_one,
        total_query_gain,
        total_key_gain,
        sum_gate,
        sum_up,
        sum_down,
        sum_gain_two,
    )


def solution(mesh):
    torus = Mesh(
        mesh.devices.reshape(mesh.shape["rep"], 4, 2, 4, mesh.shape["head"]),
        ("rep", "ctx_0", "ctx_1", "ctx_2", "head"),
    )
    return jax.shard_map(
        on_device,
        mesh=torus,
        in_specs=(
            P("rep", CTX, None),
            P("rep", CTX),
            P("rep", CTX),
            P("rep", CTX, None),
            P(CTX, "head"),
            P(CTX, "head"),
            P(CTX, "head"),
            P("head", CTX),
            P(CTX),
            P(),
            P(),
            P(CTX, "head"),
            P(CTX, "head"),
            P("head", CTX),
            P(CTX),
        ),
        out_specs=(
            P("rep", CTX, None),
            P("rep", CTX, None),
            P(CTX, "head"),
            P(CTX, "head"),
            P(CTX, "head"),
            P("head", CTX),
            P(CTX),
            P(),
            P(),
            P(CTX, "head"),
            P(CTX, "head"),
            P("head", CTX),
            P(CTX),
        ),
        check_vma=False,
    )
```

profile of v0, /device:TPU:0, one launch (start us, length us, event | category | flops | bytes accessed | tf_op | source)
XLA Modules:
  0.0 1710.8 jit_solution(11254198154008576915)
XLA Ops:
  14.9 187.2 %all-gather.3.cloned.1.call-done = bf16[1024,7682]{1,0:T(8,128)(2,1)} async-done(((bf16[32,7682]{1,0:T(8,128)(2,1)}), bf16[1024,7682]{1,0:T(8,128)(2,1)}) %all-gather.3.cloned.1.call-update) | async-done | bytes 15732752 | tf_op jit(solution)/shard_map/all_gather | solution.py:23
  220.7 4.2 fusion.69
  224.9 165.6 %all-gather.5.cloned.1.call-done = bf16[6144,1025]{1,0:T(8,128)(2,1)} async-done(((bf16[192,1025]{1,0:T(8,128)(2,1)}), bf16[6144,1025]{1,0:T(8,128)(2,1)}) %all-gather.5.cloned.1.call-update) | async-done | bytes 12595216 | tf_op jit(solution)/shard_map/all_gather | solution.py:36
  390.5 10.2 fusion.172
  400.8 9.7 reshape.494
  410.5 7.0 copy.140
  420.0 9.8 reshape.495
  429.8 7.1 copy.141
  436.8 134.3 %while.30 = (s32[]{:T(128)}, f32[4,2,192]{2,1,0:T(2,128)S(1)}, f32[4,2,192]{2,1,0:T(2,128)}, f32[4,2,192,128]{3,2,1,0:T(8,128)}, s32[12]{0:T(128)}, /*index=5*/b...) while((s32[]{:T(128)}, f32[4,2,192]{2,1,0:T(2,128)S(1)}, ...), condition=%wide.region_6.7_spmd.clone, body=%wide.region_3.6_spmd.clone.sunk | while | flops 413966528 | bytes 20079832 | solution.py:158
  576.7 4.5 all_to_all.67
  581.8 3.5 fusion.63
  585.3 4.8 fusion.108
  593.2 4.4 all_to_all.68
  604.4 175.8 %while.31 = (s32[]{:T(128)}, f32[192,4,2,128]{3,0,2,1:T(8,128)}, bf16[12,512,4,128]{3,1,2,0:T(8,128)(2,1)}, bf16[12,512,4,128]{3,1,2,0:T(8,128)(2,1)}, bf16[12,5...) while((s32[]{:T(128)}, f32[192,4,2,128]{3,0,2,1:T(8,128)}, ...), condition=%wide.region_13.14_spmd.clone, body=%wide.region_12.13_spmd.clone.sunk | while | flops 1017217728 | bytes 50466128 | solution.py:213
  780.1 10.3 copy.148
  790.4 10.3 copy.147
  800.8 9.6 copy_bitcast_fusion
  810.4 5.5 pad_maximum_fusion
  829.6 173.2 %reduce-scatter.8.cloned.1.call-done = bf16[192,1024]{1,0:T(8,128)(2,1)} async-done(((bf16[6144,1024]{1,0:T(8,128)(2,1)}), bf16[192,1024]{1,0:T(8,128)(2,1)}) %reduce-scatter.8.cloned.1.call-update) | async-done | bytes 393232 | tf_op jit(solution)/shard_map/reduce_scatter | solution.py:59
  1014.5 6.6 copy.169
  1021.4 3.8 convolution_convert_fusion.2
  1033.9 4.4 all_to_all.69
  1039.4 12.5 concatenate.38
  1053.8 3.6 fusion.103
  1058.4 4.5 all-to-all-start.1
  1062.9 80.9 %all-reduce.4 = bf16[1024]{0:T(1024)(128)(2,1)S(1)} all-reduce(bf16[1024]{0:T(1024)(128)(2,1)} %get-tuple-element.393), channel_id=7, replica_groups=mesh['rep'=2,'ctx_0'=4,'ctx_1'=2,'ctx_2'=4,'head'=2] {'ctx_0','ctx_1','c..., use_global_device_ids=true, to_apply=%region_45.46.clone | all-reduce | flops 1024 | bytes 4096
  1152.8 13.0 reduce-scatter.10.cloned.1.call-done
  1167.3 4.1 all-to-all-start.7
  1171.9 6.1 all-to-all-done.7
  1178.0 152.1 %reduce-scatter.14.cloned.1.call-done = bf16[1536,32]{0,1:T(8,128)(2,1)} async-done(((bf16[1536,1024]{0,1:T(8,128)(2,1)}), bf16[1536,32]{0,1:T(8,128)(2,1)}) %reduce-scatter.14.cloned.1.call-update) | async-done | bytes 98320 | tf_op jit(solution)/shard_map/reduce_scatter | solution.py:476
  1331.7 4.4 all-to-all-start.11
  1336.7 6.3 all-to-all-done.11
  1343.7 153.2 %reduce-scatter.16.cloned.1.call-done = bf16[32,2048]{1,0:T(8,128)(2,1)} async-done(((bf16[1024,2048]{1,0:T(8,128)(2,1)}), bf16[32,2048]{1,0:T(8,128)(2,1)}) %reduce-scatter.16.cloned.1.call-update) | async-done | bytes 131088
  1498.4 4.2 all-to-all-start.5
  1505.1 6.4 all-reduce.9
  1511.5 7.8 all-reduce.6
  1519.4 5.0 all-reduce.8
  1524.3 8.1 all-reduce.5
  1536.1 4.6 all-to-all-start.6
  1541.3 5.0 all-to-all-done.6
  1551.0 5.6 all-to-all-done.4
  1557.2 113.1 %reduce-scatter.12.cloned.1.call-done = bf16[32,3073]{1,0:T(8,128)(2,1)} async-done(((bf16[1024,3073]{1,0:T(8,128)(2,1)}), bf16[32,3073]{1,0:T(8,128)(2,1)}) %reduce-scatter.12.cloned.1.call-update) | async-done | bytes 196688 | tf_op jit(solution)/shard_map/reduce_scatter | solution.py:66
  1671.7 5.3 all-to-all-start.8
  1678.1 4.1 all-to-all-done.8
  1682.9 3.4 all-to-all-start.9
  1686.8 5.8 all-to-all-done.9
  1693.3 3.4 all-to-all-start.10
  1697.4 5.6 all-to-all-done.10
  (868 shorter events, 421.8 us)
Async XLA Ops:
  7.2 194.9 %all-gather.3.cloned.1.call-start = ((), (), s32[]{:S(2)}) async-start(), calls=%async_computation.18 | async-start | bytes 16490496 | tf_op jit(solution)/shard_map/all_gather | solution.py:23
  10.9 195.0 %copy-start.2 = (bf16[1,192,1024]{2,1,0:T(8,128)(2,1)S(1)}, bf16[1,192,1024]{2,1,0:T(8,128)(2,1)}, u32[]{:S(2)}) copy-start(bf16[1,192,1024]{2,1,0:T(8,128)(2,1)} %param.19) | copy-start | bytes 1179652
  10.9 379.6 %all-gather.5.cloned.1.call-start = ((), (), s32[]{:S(2)}) async-start(), calls=%async_computation.19 | async-start | bytes 14598144 | tf_op jit(solution)/shard_map/all_gather | solution.py:36
  12.5 194.1 %copy-start.61 = (f32[128]{0:T(128)}, f32[128]{0:T(128)S(1)}, u32[]{:S(2)}) copy-start(f32[128]{0:T(128)S(1)} %convert_element_type.294) | copy-start | bytes 1540
  14.4 189.0 %copy-start.53 = (f32[192]{0:T(256)}, f32[192]{0:T(256)S(1)}, u32[]{:S(2)}) copy-start(f32[192]{0:T(256)S(1)} %fusion.125) | copy-start | bytes 2308
  14.4 202.0 %copy-start.45 = (f32[192]{0:T(256)}, f32[192]{0:T(256)S(1)}, u32[]{:S(2)}) copy-start(f32[192]{0:T(256)S(1)} %fusion.164) | copy-start | bytes 2308
  14.8 205.3 %copy-start.20 = (f32[192,64]{1,0:T(8,128)}, f32[192,64]{1,0:T(8,128)S(1)}, u32[]{:S(2)}) copy-start(f32[192,64]{1,0:T(8,128)S(1)} %get-tuple-element.484) | copy-start | bytes 147460
  14.8 205.3 %copy-start.21 = (f32[192,64]{1,0:T(8,128)}, f32[192,64]{1,0:T(8,128)S(1)}, u32[]{:S(2)}) copy-start(f32[192,64]{1,0:T(8,128)S(1)} %get-tuple-element.485) | copy-start | bytes 147460
  205.9 10.5 copy-start.38
  210.3 792.4 %reduce-scatter.8.cloned.1.call-start = ((), (), s32[]{:S(2)}) async-start(), calls=%async_computation.20 | async-start | bytes 12976128 | tf_op jit(solution)/shard_map/reduce_scatter | solution.py:59
  211.0 8.2 copy-start.62
  574.0 7.4 copy-start.3
  574.0 16.1 slice-start
  581.2 8.8 slice-start.1
  581.6 234.4 %copy-start.50 = (f32[192]{0:T(256)}, f32[192]{0:T(256)S(1)}, u32[]{:S(2)}) copy-start(f32[192]{0:T(256)S(1)} %fusion.165) | copy-start | bytes 2308
  581.8 8.3 slice-start.2
  606.0 6.3 copy-start
  620.4 6.3 copy-start
  635.1 6.3 copy-start
  649.8 6.3 copy-start
  664.4 6.3 copy-start
  679.0 6.3 copy-start
  708.3 6.3 copy-start
  723.0 6.3 copy-start
  752.3 6.3 copy-start
  767.0 6.3 copy-start
  816.0 349.9 %reduce-scatter.10.cloned.1.call-start = ((), (), s32[]{:S(2)}) async-start(), calls=%async_computation.21 | async-start | bytes 2162688 | tf_op jit(solution)/shard_map/reduce_scatter | solution.py:458
  820.4 509.7 %reduce-scatter.14.cloned.1.call-start = ((), (), s32[]{:S(2)}) async-start(), calls=%async_computation.23 | async-start | bytes 3244032 | tf_op jit(solution)/shard_map/reduce_scatter | solution.py:476
  823.2 673.7 %reduce-scatter.16.cloned.1.call-start = ((), (), s32[]{:S(2)}) async-start(), calls=%async_computation.24 | async-start | bytes 4325376
  827.4 179.6 %copy-start.44 = (f32[192,4]{0,1:T(4,128)S(1)}, f32[192,4]{0,1:T(4,128)}, u32[]{:S(2)}) copy-start(f32[192,4]{0,1:T(4,128)} %copy-done.43) | copy-start | bytes 9220
  1021.1 649.2 %reduce-scatter.12.cloned.1.call-start = ((), (), s32[]{:S(2)}) async-start(), calls=%async_computation.22 | async-start | bytes 6758400 | tf_op jit(solution)/shard_map/reduce_scatter | solution.py:66
  1057.4 445.2 %copy-start.51 = (f32[192]{0:T(256)S(1)}, f32[192]{0:T(256)}, u32[]{:S(2)}) copy-start(f32[192]{0:T(256)} %copy-done.50) | copy-start | bytes 2308
  1058.4 285.3 %copy-start.54 = (f32[192]{0:T(256)S(1)}, f32[192]{0:T(256)}, u32[]{:S(2)}) copy-start(f32[192]{0:T(256)} %copy-done.53) | copy-start | bytes 2308
  1058.4 285.3 %copy-start.64 = (f32[192]{0:T(256)S(1)}, f32[192]{0:T(256)}, u32[]{:S(2)}) copy-start(f32[192]{0:T(256)} %get-tuple-element.398) | copy-start | bytes 2308
  1058.4 444.2 %copy-start.57 = (f32[192]{0:T(256)S(1)}, f32[192]{0:T(256)}, u32[]{:S(2)}) copy-start(f32[192]{0:T(256)} %copy-done.55) | copy-start | bytes 2308
  1058.4 85.5 %all-to-all-start.1 = ((bf16[2,192,1024]{2,1,0:T(8,128)(2,1)}), bf16[2,192,1024]{2,1,0:T(8,128)(2,1)}, u32[]{:S(2)}, u32[]{:S(2)}) async-start(bf16[2,192,1024]{2,1,0:T(8,128)(2,1)} %broadcast_in_dim.91), calls=%async_computation.1 | async-start | bytes 1572864 | tf_op jit(solution)/shard_map/all_to_all | solution.py:45
  1144.4 8.4 all-to-all-start.12
  1167.3 10.7 all-to-all-start.7
  1331.7 173.4 %copy-start.66 = (f32[128]{0:T(128)S(1)}, f32[128]{0:T(128)}, u32[]{:S(2)}) copy-start(f32[128]{0:T(128)} %get-tuple-element.391) | copy-start | bytes 1540
  1331.7 173.4 %copy-start.67 = (f32[128]{0:T(128)S(1)}, f32[128]{0:T(128)}, u32[]{:S(2)}) copy-start(f32[128]{0:T(128)} %get-tuple-element.395) | copy-start | bytes 1540
  1331.7 11.3 all-to-all-start.11
  1497.0 49.3 %slice-start.4 = ((bf16[32,2048]{1,0:T(8,128)(2,1)}), bf16[32,1024]{1,0:T(8,128)(2,1)S(1)}, s32[]{:S(2)}) async-start(bf16[32,2048]{1,0:T(8,128)(2,1)} %reduce-scatter.16.cloned.1.call-done), calls=%async_computation.29 | async-start | bytes 131072 | tf_op jit(solution)/shard_map/split | solution.py:59
  1498.4 37.0 %all-to-all-start.5 = ((bf16[2,32,512]{2,1,0:T(8,128)(2,1)}), bf16[2,32,512]{2,1,0:T(8,128)(2,1)S(1)}, u32[]{:S(2)}, u32[]{:S(2)}) async-start(bf16[2,32,512]{2,1,0:T(8,128)(2,1)} %broadcast_in_dim.101), calls=%async_computation.6 | async-start | bytes 131072 | tf_op jit(solution)/shard_map/all_to_all | solution.py:45
  1536.1 10.2 all-to-all-start.6
  1546.9 9.6 all-to-all-start.4
  1671.7 10.5 all-to-all-start.8
  1682.9 9.8 all-to-all-start.9
  1693.3 9.8 all-to-all-start.10
  (210 other events, 679.6 us)
Sparse Core Ops, SparseCore 0:
  11.1 190.9 all-gather.2
  210.5 179.9 all-gather.4
  816.1 186.6 reduce-scatter.7
  1005.0 160.7 reduce-scatter.9
  1168.2 161.8 reduce-scatter.13
  1332.3 164.5 reduce-scatter.15
  1499.4 170.9 reduce-scatter.11
where the time goes:
time: 1720 us; the launch traced here: 1710 us
  waiting for transfers between devices  999 us (58%)
  matrix products  228 us (13%)
  local copies, waits for them, and re-layouts  198 us (12%)
  blocking collectives  124 us (7%)
  other arithmetic  102 us (6%)
  starting transfers between devices  41.3 us (2%)
    all_gather x1, waiting for transfers between devices, gather_turned(): result, at, done = (lax.all_gather(both, axis, axis=0, tiled=True), 0, [])  187 us
    reduce_scatter x1, waiting for transfers between devices, side_by_side_2(): lax.psum_scatter(both, axis, scatter_dimension=dim, tiled=True)  173 us
    all_gather x1, waiting for transfers between devices, side_by_side(): result = lax.all_gather(both, axis, axis=dim, tiled=True)  166 us
    unnamed x8, waiting for transfers between devices  153 us
    reduce_scatter x1, waiting for transfers between devices, on_device(): lax.psum_scatter(grad_down.astype(jnp.bfloat16), CTX, scatter_dimension=1...  152 us
    reduce_scatter x1, waiting for transfers between devices, side_by_side_3(): lax.psum_scatter(both, axis, scatter_dimension=dim, tiled=True)  113 us
    unnamed x1, blocking collectives  80.9 us
    dynamic_slice x48, local copies, waits for them, and re-layouts, key_blocks(): final_state, ignored = lax.scan(visit_block, carried_state, blocks)  50.6 us
  transfers between devices with their start and end apart: 17, of which 15 were waited for; matrix products, arithmetic and copies ran while one was open for 6% of the time, Pallas kernels for 0%

commit v1 on v0

v1 whole, which is shorter than its diff:
```python
import math

import jax
import jax.numpy as jnp
from jax import lax
from jax.experimental import pallas as pl
from jax.experimental.pallas import tpu as pltpu
from jax.sharding import Mesh
from jax.sharding import PartitionSpec as P

MESH = pl.DeviceIdType.MESH
CTX = ("ctx_0", "ctx_1", "ctx_2")
EPSILON = 1e-06
ROPE_BASE = 1000000.0
BF = jnp.bfloat16
F32 = jnp.float32
HD = 128
D = 1024
CH = 192
HALF = 96
MIDDLE = 5952
W1C = 512
W2C = 1408
SCALE = 1.0 / math.sqrt(HD)
SCALE2 = SCALE / math.log(2.0)
VMEM_LIMIT = 56 * 1024 * 1024
PLANE = ((0, 1), (0, 3), (1, 0), (1, 1), (1, 3), (0, 2), (1, 2))
RING = (1, 3, 2)


def nn(a, b):
    return jnp.dot(a, b, preferred_element_type=F32)


def nt(a, b):
    return lax.dot_general(a, b, (((1,), (1,)), ((), ())), preferred_element_type=F32)


def tn(a, b):
    return lax.dot_general(a, b, (((0,), (0,)), ((), ())), preferred_element_type=F32)


def rcopy(src, dst, send, recv, device):
    return pltpu.make_async_remote_copy(
        src_ref=src, dst_ref=dst, send_sem=send, recv_sem=recv, device_id=device, device_id_type=MESH
    )


def place():
    return tuple(lax.axis_index(name) for name in ("ctx_0", "ctx_1", "ctx_2", "head"))


def ring_peer(z, k):
    return {"ctx_0": lax.rem(z + k, 4)}


def plane_peer(x, y, dx, dy):
    return {"ctx_1": lax.rem(x + dx, 2), "ctx_2": lax.rem(y + dy, 4)}


def greet(devices):
    barrier = pltpu.get_barrier_semaphore()
    for device in devices:
        pl.semaphore_signal(barrier, inc=1, device_id=device, device_id_type=MESH)
    pl.semaphore_wait(barrier, len(devices))


def group_devices(z, h):
    return [{"head": 1 - h}] + [ring_peer(z, k) for k in RING]


def plane_devices(x, y):
    return [plane_peer(x, y, dx, dy) for dx, dy in PLANE]


class Gather:
    def __init__(self, own, buf, z, h, sems):
        self.buf, self.z, self.h = buf, z, h
        self.sz, self.rz, self.ss, self.rs = sems
        self.sent = []
        self.from_core = {}
        self.ring = {}
        for k in RING:
            copy = rcopy(own, buf.at[z, h], self.sz.at[k], self.rz.at[k], ring_peer(z, k))
            copy.start()
            self.ring[k] = copy
            self.sent.append(copy)

    def to_core(self, k):
        source = lax.rem(self.z + 4 - k, 4)
        slot = self.buf.at[source, self.h]
        copy = rcopy(slot, slot, self.ss.at[k], self.rs.at[k], {"head": 1 - self.h})
        copy.start()
        self.from_core[k] = copy
        self.sent.append(copy)

    def forward(self, k):
        self.ring[k].wait_recv()
        self.to_core(k)

    def arrived(self, k):
        self.from_core[k].wait_recv()

    def finish(self):
        for copy in self.sent:
            copy.wait_send()


class Reduce:
    def __init__(self, parts, other, sums, inbox, z, h, sems):
        self.parts, self.other, self.sums, self.inbox, self.z, self.h = parts, other, sums, inbox, z, h
        self.ss, self.rs, self.sz, self.rz = sems
        self.sent = []
        self.core = {}
        self.ring = {}

    def give(self, k, value):
        chunk = lax.rem(self.z + k, 4)
        self.parts[chunk] = value.astype(BF).reshape(2, HALF, D)
        copy = rcopy(
            self.parts.at[chunk, 1 - self.h],
            self.other.at[chunk],
            self.ss.at[k],
            self.rs.at[k],
            {"head": 1 - self.h},
        )
        copy.start()
        self.core[k] = copy
        self.sent.append(copy)

    def pass_on(self, k):
        chunk = lax.rem(self.z + k, 4)
        self.core[k].wait_recv()
        both = self.parts[chunk, self.h].astype(F32) + self.other[chunk].astype(F32)
        self.sums[chunk] = both.astype(BF)
        copy = rcopy(
            self.sums.at[chunk],
            self.inbox.at[self.z],
            self.sz.at[k],
            self.rz.at[k],
            ring_peer(self.z, k),
        )
        copy.start()
        self.ring[k] = copy
        self.sent.append(copy)

    def total(self):
        self.core[0].wait_recv()
        result = self.parts[self.z, self.h].astype(F32) + self.other[self.z].astype(F32)
        for k in RING:
            self.ring[k].wait_recv()
            result += self.inbox[lax.rem(self.z + 4 - k, 4)].astype(F32)
        return result

    def finish(self):
        for copy in self.sent:
            copy.wait_send()


def reduce_scratch():
    return [
        pltpu.VMEM((4, 2, HALF, D), BF),
        pltpu.VMEM((4, HALF, D), BF),
        pltpu.VMEM((4, HALF, D), BF),
        pltpu.VMEM((4, HALF, D), BF),
    ] + [pltpu.SemaphoreType.DMA((4,))] * 4


def gather_scratch():
    return [pltpu.SemaphoreType.DMA((4,))] * 4


def spread_kernel(
    tok, cot, w1, w2, gains, tok_all, cot_all, w1_all, w2_ring, gains_all,
    w1_ring, gains_ring, local, ring_send, ring_recv, plane_send, plane_recv,
    ts0, ts1, ts2, ts3, cs0, cs1, cs2, cs3,
):
    z, x, y, h = place()
    t = x * 4 + y
    greet(group_devices(z, h) + plane_devices(x, y))
    locals_ = [
        pltpu.make_async_copy(w1.at[z], w1_ring.at[z], local.at[0]),
        pltpu.make_async_copy(gains, gains_ring.at[z], local.at[1]),
        pltpu.make_async_copy(w2.at[z], w2_ring.at[z], local.at[2]),
        pltpu.make_async_copy(tok, tok_all.at[z], local.at[3]),
        pltpu.make_async_copy(cot, cot_all.at[z], local.at[4]),
    ]
    for copy in locals_:
        copy.start()
    sent = []
    ring = []
    for k in RING:
        peer = lax.rem(z + k, 4)
        pair = [
            rcopy(w1.at[peer], w1_ring.at[z], ring_send.at[0, k], ring_recv.at[0, k], ring_peer(z, k)),
            rcopy(gains, gains_ring.at[z], ring_send.at[1, k], ring_recv.at[1, k], ring_peer(z, k)),
        ]
        for copy in pair:
            copy.start()
        ring += pair
    tokens_out = Gather(tok.at[h], tok_all, z, h, (ts0, ts1, ts2, ts3))
    locals_[0].wait()
    locals_[1].wait()
    for copy in ring:
        copy.wait_recv()
    plane = []
    for n, (dx, dy) in enumerate(PLANE):
        device = plane_peer(x, y, dx, dy)
        pair = [
            rcopy(w1_ring, w1_all.at[:, t], plane_send.at[0, n], plane_recv.at[0, n], device),
            rcopy(gains_ring, gains_all.at[:, t], plane_send.at[1, n], plane_recv.at[1, n], device),
        ]
        for copy in pair:
            copy.start()
        plane += pair
    keep = [
        pltpu.make_async_copy(w1_ring, w1_all.at[:, t], local.at[5]),
        pltpu.make_async_copy(gains_ring, gains_all.at[:, t], local.at[6]),
    ]
    for copy in keep:
        copy.start()
    second = []
    for k in RING:
        peer = lax.rem(z + k, 4)
        copy = rcopy(w2.at[peer], w2_ring.at[z], ring_send.at[2, k], ring_recv.at[2, k], ring_peer(z, k))
        copy.start()
        second.append(copy)
    cot_out = Gather(cot.at[h], cot_all, z, h, (cs0, cs1, cs2, cs3))
    for k in RING:
        tokens_out.forward(k)
    for k in RING:
        cot_out.forward(k)
    for k in RING:
        tokens_out.arrived(k)
        cot_out.arrived(k)
    for copy in ring + plane + second:
        copy.wait_send()
    for copy in plane + second:
        copy.wait_recv()
    tokens_out.finish()
    cot_out.finish()
    for copy in locals_[2:] + keep:
        copy.wait()


def spread(tok, cot, w1, w2, gains):
    any_ = pl.BlockSpec(memory_space=pl.ANY)
    return pl.pallas_call(
        spread_kernel,
        out_shape=(
            jax.ShapeDtypeStruct((4, 2, HALF, D), BF),
            jax.ShapeDtypeStruct((4, 2, HALF, D), BF),
            jax.ShapeDtypeStruct((4, 8, 32, W1C), BF),
            jax.ShapeDtypeStruct((4, 32, W2C), BF),
            jax.ShapeDtypeStruct((4, 8, 8, 128), F32),
        ),
        in_specs=[any_] * 5,
        out_specs=(any_,) * 5,
        scratch_shapes=[
            pltpu.VMEM((4, 32, W1C), BF),
            pltpu.VMEM((4, 8, 128), F32),
            pltpu.SemaphoreType.DMA((7,)),
            pltpu.SemaphoreType.DMA((3, 4)),
            pltpu.SemaphoreType.DMA((3, 4)),
            pltpu.SemaphoreType.DMA((2, 7)),
            pltpu.SemaphoreType.DMA((2, 7)),
        ]
        + gather_scratch()
        + gather_scratch(),
        compiler_params=pltpu.CompilerParams(
            collective_id=0, has_side_effects=True, vmem_limit_bytes=VMEM_LIMIT
        ),
        name="spread",
    )(tok, cot, w1, w2, gains)


def turn(u, cosine, sine):
    return u * cosine + pltpu.roll(u, HD // 2, 1) * sine


def rms_rate(v):
    return lax.rsqrt(jnp.mean(v * v, axis=-1, keepdims=True) + EPSILON)


def heads_kernel(tok, w1, gain, qgain, kgain, cosine, sine, q, kv, pre, normed):
    v = tok[...].astype(F32)
    n = (v * rms_rate(v) * gain[...]).astype(BF)
    normed[...] = n
    out = nn(n, w1[...])
    pre[...] = out[:, :384]
    c, s = cosine[...], sine[...]
    for i in range(3):
        u = out[:, i * HD : (i + 1) * HD]
        u = turn(u * rms_rate(u) * (qgain if i < 2 else kgain)[...], c, s).astype(BF)
        if i < 2:
            q[0, i * CH : (i + 1) * CH, :] = u
        else:
            kv[0, :, :HD] = u
    kv[0, :, HD:] = out[:, 384:].astype(BF)


def make_heads(tok_all, w1, gain, qgain, kgain, cosine, sine):
    def whole(*shape):
        return pl.BlockSpec(shape, lambda i: (0,) * len(shape))

    return pl.pallas_call(
        heads_kernel,
        grid=(4,),
        out_shape=(
            jax.ShapeDtypeStruct((4, 2 * CH, HD), BF),
            jax.ShapeDtypeStruct((4, CH, 2 * HD), BF),
            jax.ShapeDtypeStruct((4 * CH, 384), F32),
            jax.ShapeDtypeStruct((4 * CH, D), BF),
        ),
        in_specs=[
            pl.BlockSpec((CH, D), lambda i: (i, 0)),
            whole(D, W1C),
            whole(1, D),
            whole(1, HD),
            whole(1, HD),
            pl.BlockSpec((CH, HD), lambda i: (i, 0)),
            pl.BlockSpec((CH, HD), lambda i: (i, 0)),
        ],
        out_specs=(
            pl.BlockSpec((1, 2 * CH, HD), lambda i: (i, 0, 0)),
            pl.BlockSpec((1, CH, 2 * HD), lambda i: (i, 0, 0)),
            pl.BlockSpec((CH, 384), lambda i: (i, 0)),
            pl.BlockSpec((CH, D), lambda i: (i, 0)),
        ),
        compiler_params=pltpu.CompilerParams(vmem_limit_bytes=VMEM_LIMIT),
        name="make_heads",
    )(tok_all, w1, gain, qgain, kgain, cosine, sine)


def query_index(chunk):
    lane = lax.broadcasted_iota(jnp.int32, (1, 2 * CH), 1)
    return chunk * CH + jnp.where(lane < CH, lane, lane - CH)


def first_allowed(index, start):
    return jnp.where(index < start, 0, jnp.where(index < start + MIDDLE, start, start + MIDDLE))


def key_index(chunk):
    return chunk * CH + lax.broadcasted_iota(jnp.int32, (CH, 1), 0)


def row_sums(p):
    return jnp.sum(p.reshape(CH // 8, 8, 2 * CH), axis=0)


def attend_kernel(
    q, kv, w2_ring, start_ref, att, out_t, logs, kv_all, w2_all, acc, den,
    local, kv_send, kv_recv, w_send, w_recv,
):
    z, x, y, h = place()
    t = x * 4 + y
    greet(plane_devices(x, y))
    copies = []
    weights = []
    for n, (dx, dy) in enumerate(PLANE):
        copy = rcopy(kv, kv_all.at[:, t], kv_send.at[n], kv_recv.at[n], plane_peer(x, y, dx, dy))
        copy.start()
        copies.append(copy)
    for n, (dx, dy) in enumerate(PLANE):
        copy = rcopy(w2_ring, w2_all.at[:, t], w_send.at[n], w_recv.at[n], plane_peer(x, y, dx, dy))
        copy.start()
        weights.append(copy)
    keep = pltpu.make_async_copy(w2_ring, w2_all.at[:, t], local.at[0])
    keep.start()
    kv_all[:, t] = kv[...]
    start = start_ref[0, 0]
    for copy in copies:
        copy.wait_recv()

    def block(j, qc):
        k, v = kv_all[j // 8, lax.rem(j, 8), :, :HD], kv_all[j // 8, lax.rem(j, 8), :, HD:]
        return jnp.exp2(nt(k, qc) * SCALE2), v

    for c in range(4):
        qc = q[c]
        mine = c * 8 + t
        index = query_index(mine)
        lowest = first_allowed(index, start)
        acc[...] = jnp.zeros_like(acc)
        den[...] = jnp.zeros_like(den)

        def several(first, count):
            a, d = None, None
            for u in range(count):
                p, v = block(first + u, qc)
                dd = row_sums(p)
                aa = tn(v, p.astype(BF))
                a = aa if a is None else a + aa
                d = dd if d is None else d + dd
            acc[...] += a
            den[...] += d

        plain = lax.max(mine - 1, 0)
        fours = plain // 4

        @pl.loop(0, fours)
        def _(i):
            several(1 + 4 * i, 4)

        @pl.loop(1 + 4 * fours, 1 + plain)
        def _(j):
            several(j, 1)

        inside = (index < start + MIDDLE).astype(F32)
        total = acc[...] * inside
        denominator = jnp.sum(den[...], axis=0, keepdims=True) * inside
        last = key_index(mine)
        p, v = block(mine, qc)
        p = jnp.where((last <= index) & (last >= lowest), p, 0.0)
        total += tn(v, p.astype(BF))
        denominator += jnp.sum(p, axis=0, keepdims=True)
        p, v = block(0, qc)
        low = key_index(0)
        p = jnp.where(low >= jnp.where(mine > 0, lowest, 1 << 30), p, 0.0)
        total += tn(v, p.astype(BF))
        denominator += jnp.sum(p, axis=0, keepdims=True)
        total = total / denominator
        out_t[c] = total
        logs[c] = jnp.log2(denominator)
        rows = total.T.astype(BF)
        att[c, :, :HD] = rows[:CH]
        att[c, :, HD:] = rows[CH:]
    for copy in copies + weights:
        copy.wait_send()
    for copy in weights:
        copy.wait_recv()
    keep.wait()


def attend(q, kv, w2_ring, start):
    any_ = pl.BlockSpec(memory_space=pl.ANY)
    vmem = pl.BlockSpec(memory_space=pltpu.VMEM)
    smem = pl.BlockSpec(memory_space=pltpu.SMEM)
    return pl.pallas_call(
        attend_kernel,
        out_shape=(
            jax.ShapeDtypeStruct((4, CH, 2 * HD), BF),
            jax.ShapeDtypeStruct((4, HD, 2 * CH), F32),
            jax.ShapeDtypeStruct((4, 1, 2 * CH), F32),
            jax.ShapeDtypeStruct((4, 8, CH, 2 * HD), BF),
            jax.ShapeDtypeStruct((4, 8, 32, W2C), BF),
        ),
        in_specs=[vmem, vmem, any_, smem],
        out_specs=(vmem, vmem, vmem, vmem, any_),
        scratch_shapes=[
            pltpu.VMEM((HD, 2 * CH), F32),
            pltpu.VMEM((8, 2 * CH), F32),
            pltpu.SemaphoreType.DMA((1,)),
            pltpu.SemaphoreType.DMA((7,)),
            pltpu.SemaphoreType.DMA((7,)),
            pltpu.SemaphoreType.DMA((7,)),
            pltpu.SemaphoreType.DMA((7,)),
        ],
        compiler_params=pltpu.CompilerParams(
            collective_id=1, has_side_effects=True, vmem_limit_bytes=VMEM_LIMIT
        ),
        name="attend",
    )(q, kv, w2_ring, start)


def middle_kernel(
    att, w2, gain, tok_all, cot_all, res, grad_hidden, grad_att, dw, gain_term,
    n2, gh, act, ggu, hidden, *scratch,
):
    first = scratch[0:8]
    down = scratch[8:16]
    back = scratch[16:24]
    fwd_sems = scratch[24:28]
    bwd_sems = scratch[28:32]
    res_send, res_recv = scratch[32:34]
    z, x, y, h = place()
    greet(group_devices(z, h))
    out_sum = Reduce(*first[:4], z, h, first[4:])
    for k in (1, 3, 2, 0):
        out_sum.give(k, nt(att[lax.rem(z + k, 4)], w2[:, 768:1024]))
    for k in RING:
        out_sum.pass_on(k)
    v = tok_all[z, h].astype(F32) + out_sum.total()
    hidden[...] = v
    g = gain[...]
    rate = rms_rate(v)
    n2[z, h] = (v * rate * g).astype(BF)
    n2_out = Gather(n2.at[z, h], n2, z, h, fwd_sems)
    n2_out.to_core(0)
    down_sum = Reduce(*down[:4], z, h, down[4:])
    back_sum = Reduce(*back[:4], z, h, back[4:])

    def feed(k):
        chunk = lax.rem(z + 4 - k, 4)
        back_k = (4 - k) % 4
        rows = n2[chunk].reshape(CH, D)
        gu = nn(rows, w2[:, :768])
        ga = nn(cot_all[chunk].reshape(CH, D), w2[:, 1024:])
        gate, up = gu[:, :384], gu[:, 384:]
        s = 1.0 / (1.0 + jnp.exp(-gate))
        silu = gate * s
        a = (silu * up).astype(BF)
        act[chunk] = a
        down_sum.give(back_k, nt(a, w2[:, 1024:]))
        gg = (ga * up * s * (1.0 + gate * (1.0 - s))).astype(BF)
        gp = (ga * silu).astype(BF)
        ggu[chunk, :, :384] = gg
        ggu[chunk, :, 384:] = gp
        back_sum.give(back_k, nt(ggu[chunk], w2[:, :768]))

    n2_out.arrived(0)
    feed(0)
    n2_out.forward(1)
    n2_out.forward(3)
    n2_out.arrived(1)
    feed(1)
    n2_out.forward(2)
    n2_out.arrived(3)
    back_sum.pass_on(3)
    feed(3)
    back_sum.pass_on(1)
    n2_out.arrived(2)
    feed(2)
    back_sum.pass_on(2)
    down_sum.pass_on(3)
    down_sum.pass_on(1)
    down_sum.pass_on(2)
    gy = back_sum.total()
    v = hidden[...]
    rate = rms_rate(v)
    vr = v * rate
    gain_term[...] = jnp.sum(gy * vr, axis=0, keepdims=True)
    gg = gy * g
    gv = rate * (gg - vr * jnp.mean(gg * vr, axis=-1, keepdims=True))
    grad = cot_all[z, h].astype(F32) + gv
    grad_hidden[...] = grad
    gh[z, h] = grad.astype(BF)
    gh_out = Gather(gh.at[z, h], gh, z, h, bwd_sems)
    gh_out.to_core(0)
    res[h] = (hidden[...] + down_sum.total()).astype(BF)
    res_out = rcopy(res.at[h], res.at[h], res_send.at[0], res_recv.at[0], {"head": 1 - h})
    res_out.start()
    dw[:, :768] = tn(n2[...].reshape(4 * CH, D), ggu[...].reshape(4 * CH, 768)).astype(BF)
    for k in RING:
        gh_out.forward(k)
    dw[:, 1024:] = tn(cot_all[...].reshape(4 * CH, D), act[...].reshape(4 * CH, 384)).astype(BF)
    for k in range(4):
        gh_out.arrived(k)
    full = gh[...].reshape(4 * CH, D)
    ga = nn(full, w2[:, 768:1024]).astype(BF)
    for c in range(4):
        for i in range(2):
            grad_att[c, i * CH : (i + 1) * CH, :] = ga[c * CH : (c + 1) * CH, i * HD : (i + 1) * HD]
    dw[:, 768:1024] = tn(full, att[...].reshape(4 * CH, 256)).astype(BF)
    res_out.wait()
    for item in (out_sum, down_sum, back_sum, n2_out, gh_out):
        item.finish()


def middle(att, w2, gain, tok_all, cot_all):
    vmem = pl.BlockSpec(memory_space=pltpu.VMEM)
    return pl.pallas_call(
        middle_kernel,
        out_shape=(
            jax.ShapeDtypeStruct((2, HALF, D), BF),
            jax.ShapeDtypeStruct((HALF, D), F32),
            jax.ShapeDtypeStruct((4, 2 * CH, HD), BF),
            jax.ShapeDtypeStruct((D, W2C), BF),
            jax.ShapeDtypeStruct((1, D), F32),
        ),
        in_specs=[vmem] * 5,
        out_specs=(vmem,) * 5,
        scratch_shapes=[
            pltpu.VMEM((4, 2, HALF, D), BF),
            pltpu.VMEM((4, 2, HALF, D), BF),
            pltpu.VMEM((4, CH, 384), BF),
            pltpu.VMEM((4, CH, 768), BF),
            pltpu.VMEM((HALF, D), F32),
        ]
        + reduce_scratch() * 3
        + gather_scratch() * 2
        + [pltpu.SemaphoreType.DMA((1,))] * 2,
        compiler_params=pltpu.CompilerParams(
            collective_id=2, has_side_effects=True, vmem_limit_bytes=VMEM_LIMIT
        ),
        name="middle",
    )(att, w2, gain, tok_all, cot_all)


def attend_back_kernel(
    q, kv_all, go, out_t, logs, dw, start_ref, dq, dkv, dw_sum,
    dq_t, delta, far, acc, give, take, dw_take, give_send, give_recv, dw_send, dw_recv,
):
    z, x, y, h = place()
    t = x * 4 + y
    greet(plane_devices(x, y))
    weights = []
    for n, (dx, dy) in enumerate(PLANE):
        peer = lax.rem(x + dx, 2) * 4 + lax.rem(y + dy, 4)
        copy = rcopy(dw.at[:, peer], dw_take.at[n], dw_send.at[n], dw_recv.at[n], plane_peer(x, y, dx, dy))
        copy.start()
        weights.append(copy)
    start = start_ref[0, 0]
    dq_t[...] = jnp.zeros_like(dq_t)
    for c in range(4):
        delta[c] = jnp.sum(out_t[c] * go[c].astype(F32).T, axis=0, keepdims=True)
        far[c] = jnp.where(query_index(c * 8 + t) < start + MIDDLE, logs[c], 1e30)

    def pair(c, k, v, log, keep):
        qc, g = q[c], go[c]
        p = jnp.exp2(nt(k, qc) * SCALE2 - log)
        if keep is not None:
            p = jnp.where(keep, p, 0.0)
        ds = (p * (nt(v, g) - delta[c])).astype(BF)
        dq_t[c] += tn(k, ds)
        return nn(ds, qc), nn(p.astype(BF), g)

    def keys_of(other, own):
        result = []
        for c in range(4):
            both = kv_all[c, other]
            k, v = both[:, :HD], both[:, HD:]
            index = key_index(c * 8 + other)
            late = index >= start if c == 0 else None
            if own:
                mine = query_index(c * 8 + t)
                keep = (index <= mine) & (index >= first_allowed(mine, start))
                dk, dv = pair(c, k, v, logs[c], keep)
                acc[:, :HD] = dk
                acc[:, HD:] = dv
            else:
                acc[...] = jnp.zeros_like(acc)

                @pl.when(other < t)
                def _():
                    dk, dv = pair(c, k, v, far[c], late)
                    acc[:, :HD] = dk
                    acc[:, HD:] = dv

            dk, dv = acc[:, :HD], acc[:, HD:]
            for later in range(c + 1, 4):
                a, b = pair(later, k, v, far[later], late)
                dk += a
                dv += b
            result.append((dk * SCALE, dv))
        return result

    sent = []
    for n, (dx, dy) in enumerate(PLANE):
        other = lax.rem(x + dx, 2) * 4 + lax.rem(y + dy, 4)
        for c, (dk, dv) in enumerate(keys_of(other, False)):
            give[n, c, :, :HD] = dk.astype(BF)
            give[n, c, :, HD:] = dv.astype(BF)
        copy = rcopy(give.at[n], take.at[n], give_send.at[n], give_recv.at[n], plane_peer(x, y, dx, dy))
        copy.start()
        sent.append(copy)
    for c, (dk, dv) in enumerate(keys_of(t, True)):
        dkv[c, :, :HD] = dk
        dkv[c, :, HD:] = dv
    for c in range(4):
        dq[c] = (dq_t[c] * SCALE).T
    for copy in weights:
        copy.wait()
    for c in range(4):
        part = dw[c, t].astype(F32)
        for n in range(7):
            part += dw_take[n, c].astype(F32)
        dw_sum[c] = part.astype(BF)
    for copy in sent:
        copy.wait()
    for c in range(4):
        part = dkv[c]
        for n in range(7):
            part += take[n, c].astype(F32)
        dkv[c] = part


def attend_back(q, kv_all, go, out_t, logs, dw, start):
    vmem = pl.BlockSpec(memory_space=pltpu.VMEM)
    smem = pl.BlockSpec(memory_space=pltpu.SMEM)
    return pl.pallas_call(
        attend_back_kernel,
        out_shape=(
            jax.ShapeDtypeStruct((4, 2 * CH, HD), F32),
            jax.ShapeDtypeStruct((4, CH, 2 * HD), F32),
            jax.ShapeDtypeStruct((4, 32, W2C), BF),
        ),
        in_specs=[vmem] * 6 + [smem],
        out_specs=(vmem,) * 3,
        scratch_shapes=[
            pltpu.VMEM((4, HD, 2 * CH), F32),
            pltpu.VMEM((4, 1, 2 * CH), F32),
            pltpu.VMEM((4, 1, 2 * CH), F32),
            pltpu.VMEM((CH, 2 * HD), F32),
            pltpu.VMEM((7, 4, CH, 2 * HD), BF),
            pltpu.VMEM((7, 4, CH, 2 * HD), BF),
            pltpu.VMEM((7, 4, 32, W2C), BF),
            pltpu.SemaphoreType.DMA((7,)),
            pltpu.SemaphoreType.DMA((7,)),
            pltpu.SemaphoreType.DMA((7,)),
            pltpu.SemaphoreType.DMA((7,)),
        ],
        compiler_params=pltpu.CompilerParams(
            collective_id=3, has_side_effects=True, vmem_limit_bytes=VMEM_LIMIT
        ),
        name="attend_back",
    )(q, kv_all, go, out_t, logs, dw, start)


def finish_kernel(
    dq, dkv, pre, normed, w1, gain, qgain, kgain, cosine, sine, tok_all, grad_hidden, dw2, gain_two,
    ig, g1, g2, terms_out,
    dpre, dw1, take, ring1, ring2, twin1, twin2, dw1_sum, term, term_core, term_plane, term_ring, term_twin, *scratch,
):
    sums = scratch[0:8]
    plane_send, plane_recv, ring_send, ring_recv, twin_send, twin_recv, ig_send, ig_recv, term_send, term_recv = scratch[8:]
    z, x, y, h = place()
    t = x * 4 + y
    twin = {"rep": 1 - lax.axis_index("rep")}
    greet(group_devices(z, h) + plane_devices(x, y) + [twin])

    def around(source, ring, which):
        copies = []
        for k in RING:
            copy = rcopy(
                source.at[lax.rem(z + k, 4)],
                ring.at[z],
                ring_send.at[which, k],
                ring_recv.at[which, k],
                ring_peer(z, k),
            )
            copy.start()
            copies.append(copy)
        ring[z] = source[z]
        return copies

    copies2 = around(dw2, ring2, 1)
    c_, s_ = cosine[...], sine[...]
    heads = []
    for i in range(2):
        heads.append(jnp.concatenate([dq[c, i * CH : (i + 1) * CH, :] for c in range(4)], axis=0))
    heads.append(dkv[...].reshape(4 * CH, 2 * HD)[:, :HD])
    terms = []
    for i, dy in enumerate(heads):
        gy = turn(dy, c_, -s_)
        v = pre[:, i * HD : (i + 1) * HD]
        rate = rms_rate(v)
        vr = v * rate
        terms.append(jnp.sum(gy * vr, axis=0, keepdims=True))
        gg = gy * (qgain if i < 2 else kgain)[...]
        out = rate * (gg - vr * jnp.mean(gg * vr, axis=-1, keepdims=True))
        dpre[:, i * HD : (i + 1) * HD] = out.astype(BF)
    dpre[:, 3 * HD :] = dkv[...].reshape(4 * CH, 2 * HD)[:, HD:].astype(BF)
    term[...] = jnp.zeros_like(term)
    term[16:17] = terms[0] + terms[1]
    term[17:18] = terms[2]
    dw1[...] = tn(normed[...], dpre[...]).astype(BF).reshape(4, 8, 32, W1C)
    plane = []
    for n, (dx, dy) in enumerate(PLANE):
        peer = lax.rem(x + dx, 2) * 4 + lax.rem(y + dy, 4)
        copy = rcopy(
            dw1.at[:, peer], take.at[n], plane_send.at[n], plane_recv.at[n], plane_peer(x, y, dx, dy)
        )
        copy.start()
        plane.append(copy)
    norm_sum = Reduce(*sums[:4], z, h, sums[4:])
    for k in (1, 3, 2, 0):
        chunk = lax.rem(z + k, 4)
        norm_sum.give(k, nt(dpre[pl.ds(pl.multiple_of(chunk * CH, CH), CH), :], w1[...]))
    for k in RING:
        norm_sum.pass_on(k)
    for copy in copies2:
        copy.wait()
    twin_copy2 = rcopy(ring2, twin2, twin_send.at[1], twin_recv.at[1], twin)
    twin_copy2.start()
    gy = norm_sum.total()
    v = tok_all[z, h].astype(F32)
    rate = rms_rate(v)
    vr = v * rate
    own_term = jnp.sum(gy * vr, axis=0, keepdims=True)
    for i in range(8):
        term[i : i + 1] = own_term[:, i * HD : (i + 1) * HD]
        term[8 + i : 9 + i] = gain_two[:, i * HD : (i + 1) * HD]
    term_copy = rcopy(term, term_core, term_send.at[0], term_recv.at[0], {"head": 1 - h})
    term_copy.start()
    gg = gy * gain[...]
    gv = rate * (gg - vr * jnp.mean(gg * vr, axis=-1, keepdims=True))
    ig[h] = (grad_hidden[...] + gv).astype(BF)
    ig_out = rcopy(ig.at[h], ig.at[h], ig_send.at[0], ig_recv.at[0], {"head": 1 - h})
    ig_out.start()
    term_copy.wait()
    term[...] += term_core[...]
    term_copies = []
    for n, (dx, dy) in enumerate(PLANE):
        copy = rcopy(term, term_plane.at[n], term_send.at[1 + n], term_recv.at[1 + n], plane_peer(x, y, dx, dy))
        copy.start()
        term_copies.append(copy)
    for copy in plane:
        copy.wait()
    part = dw1[:, t].astype(F32)
    for n in range(7):
        part += take[n].astype(F32)
    dw1_sum[...] = part.astype(BF)
    copies1 = around(dw1_sum, ring1, 0)
    for copy in term_copies:
        copy.wait()
    for n in range(7):
        term[...] += term_plane[n]
    term_copies = []
    for k in RING:
        copy = rcopy(term, term_ring.at[k - 1], term_send.at[7 + k], term_recv.at[7 + k], ring_peer(z, k))
        copy.start()
        term_copies.append(copy)
    for copy in copies1:
        copy.wait()
    twin_copy1 = rcopy(ring1, twin1, twin_send.at[0], twin_recv.at[0], twin)
    twin_copy1.start()
    for copy in term_copies:
        copy.wait()
    for k in range(3):
        term[...] += term_ring[k]
    term_copy = rcopy(term, term_twin, term_send.at[11], term_recv.at[11], twin)
    term_copy.start()
    twin_copy2.wait()
    g2[...] = ring2[...].astype(F32) + twin2[...].astype(F32)
    twin_copy1.wait()
    g1[...] = ring1[...].astype(F32) + twin1[...].astype(F32)
    ig_out.wait()
    term_copy.wait()
    terms_out[...] = term[...] + term_twin[...]
    norm_sum.finish()


def finish(dq, dkv, pre, normed, w1, gain, qgain, kgain, cosine, sine, tok_all, grad_hidden, dw2, gain_two):
    vmem = pl.BlockSpec(memory_space=pltpu.VMEM)
    return pl.pallas_call(
        finish_kernel,
        out_shape=(
            jax.ShapeDtypeStruct((2, HALF, D), BF),
            jax.ShapeDtypeStruct((4, 32, W1C), F32),
            jax.ShapeDtypeStruct((4, 32, W2C), F32),
            jax.ShapeDtypeStruct((24, HD), F32),
        ),
        in_specs=[vmem] * 14,
        out_specs=(vmem,) * 4,
        scratch_shapes=[
            pltpu.VMEM((4 * CH, W1C), BF),
            pltpu.VMEM((4, 8, 32, W1C), BF),
            pltpu.VMEM((7, 4, 32, W1C), BF),
            pltpu.VMEM((4, 32, W1C), BF),
            pltpu.VMEM((4, 32, W2C), BF),
            pltpu.VMEM((4, 32, W1C), BF),
            pltpu.VMEM((4, 32, W2C), BF),
            pltpu.VMEM((4, 32, W1C), BF),
            pltpu.VMEM((24, HD), F32),
            pltpu.VMEM((24, HD), F32),
            pltpu.VMEM((7, 24, HD), F32),
            pltpu.VMEM((3, 24, HD), F32),
            pltpu.VMEM((24, HD), F32),
        ]
        + reduce_scratch()
        + [
            pltpu.SemaphoreType.DMA((7,)),
            pltpu.SemaphoreType.DMA((7,)),
            pltpu.SemaphoreType.DMA((2, 4)),
            pltpu.SemaphoreType.DMA((2, 4)),
            pltpu.SemaphoreType.DMA((2,)),
            pltpu.SemaphoreType.DMA((2,)),
            pltpu.SemaphoreType.DMA((1,)),
            pltpu.SemaphoreType.DMA((1,)),
            pltpu.SemaphoreType.DMA((12,)),
            pltpu.SemaphoreType.DMA((12,)),
        ],
        compiler_params=pltpu.CompilerParams(
            collective_id=4, has_side_effects=True, vmem_limit_bytes=VMEM_LIMIT
        ),
        name="finish",
    )(dq, dkv, pre, normed, w1, gain, qgain, kgain, cosine, sine, tok_all, grad_hidden, dw2, gain_two)


def on_device(
    tokens, segments, positions, cotangent, query_weight, key_weight, value_weight, out_weight,
    attn_gain, query_gain, key_gain, gate_weight, up_weight, down_weight, mlp_gain,
):
    t = lax.axis_index("ctx_1") * 4 + lax.axis_index("ctx_2")
    own_index = lax.axis_index(CTX) * CH + jnp.arange(CH, dtype=jnp.int32)
    start = jnp.max(jnp.where(segments[0] == 1, own_index - positions[0], 0))
    group = ((jnp.arange(4, dtype=jnp.int32) * 8 + t)[:, None] * CH + jnp.arange(CH, dtype=jnp.int32)).reshape(-1)
    begin = jnp.where(group < start, 0, jnp.where(group < start + MIDDLE, start, start + MIDDLE))
    inverse = ROPE_BASE ** (-jnp.arange(HD // 2, dtype=F32) / (HD // 2))
    angles = (group - begin).astype(F32)[:, None] * inverse[None, :]
    cosine, sine = jnp.cos(angles), jnp.sin(angles)
    cosine = jnp.concatenate([cosine, cosine], axis=1)
    sine = jnp.concatenate([-sine, sine], axis=1)

    def shards(w):
        return w.reshape(32, 4, -1)

    w1 = jnp.concatenate([shards(query_weight), shards(key_weight), shards(value_weight)], axis=2)
    w2 = jnp.concatenate(
        [shards(gate_weight), shards(up_weight), shards(out_weight.T), shards(down_weight.T)], axis=2
    )
    gains = jnp.concatenate([attn_gain, mlp_gain, jnp.zeros((64,), BF)]).astype(F32)
    gains = jnp.broadcast_to(gains[None], (8, 128))
    tok_all, cot_all, w1_all, w2_ring, gains_all = spread(
        tokens.reshape(2, HALF, D),
        cotangent.reshape(2, HALF, D),
        w1.transpose(1, 0, 2),
        w2.transpose(1, 0, 2),
        gains,
    )
    gain_one = gains_all[:, :, 0, :32].reshape(1, D)
    gain_two = gains_all[:, :, 0, 32:64].reshape(1, D)
    w1_all = w1_all.reshape(D, W1C)
    qgain, kgain = query_gain.astype(F32)[None], key_gain.astype(F32)[None]
    q, kv, pre, normed = make_heads(
        tok_all.reshape(4 * CH, D), w1_all, gain_one, qgain, kgain, cosine, sine
    )
    start = start.reshape(1, 1)
    att, out_t, logs, kv_all, w2_all = attend(q, kv, w2_ring, start)
    result, grad_hidden, grad_att, dw2, gain_two_term = middle(
        att, w2_all.reshape(D, W2C), gain_two, tok_all, cot_all
    )
    dq, dkv, dw2_sum = attend_back(q, kv_all, grad_att, out_t, logs, dw2.reshape(4, 8, 32, W2C), start)
    input_grad, g1, g2, terms = finish(
        dq, dkv, pre, normed, w1_all, gain_one, qgain, kgain, cosine, sine, tok_all, grad_hidden, dw2_sum,
        gain_two_term,
    )
    terms = terms.reshape(-1)
    own = lax.axis_index(CTX) * 32

    def joined(g, a, b):
        return g[:, :, a:b].transpose(1, 0, 2).reshape(32, -1)

    return (
        result.reshape(1, CH, D),
        input_grad.reshape(1, CH, D),
        joined(g1, 0, 256),
        joined(g1, 256, 384),
        joined(g1, 384, 512),
        joined(g2, 768, 1024).T,
        lax.dynamic_slice(terms, (own,), (32,)),
        terms[2 * D : 2 * D + HD],
        terms[2 * D + HD : 2 * D + 2 * HD],
        joined(g2, 0, 384),
        joined(g2, 384, 768),
        joined(g2, 1024, 1408).T,
        lax.dynamic_slice(terms, (D + own,), (32,)),
    )


def solution(mesh):
    torus = Mesh(
        mesh.devices.reshape(mesh.shape["rep"], 4, 2, 4, mesh.shape["head"]),
        ("rep", "ctx_0", "ctx_1", "ctx_2", "head"),
    )
    return jax.shard_map(
        on_device,
        mesh=torus,
        in_specs=(
            P("rep", CTX, None),
            P("rep", CTX),
            P("rep", CTX),
            P("rep", CTX, None),
            P(CTX, "head"),
            P(CTX, "head"),
            P(CTX, "head"),
            P("head", CTX),
            P(CTX),
            P(),
            P(),
            P(CTX, "head"),
            P(CTX, "head"),
            P("head", CTX),
            P(CTX),
        ),
        out_specs=(
            P("rep", CTX, None),
            P("rep", CTX, None),
            P(CTX, "head"),
            P(CTX, "head"),
            P(CTX, "head"),
            P("head", CTX),
            P(CTX),
            P(),
            P(),
            P(CTX, "head"),
            P(CTX, "head"),
            P("head", CTX),
            P(CTX),
        ),
        check_vma=False,
    )
```

time: 1720 us -> 329 us (0.19)
  waiting for transfers between devices: 999 us -> 0 us
  Pallas kernels: 0 us -> 299 us
  matrix products: 228 us -> 0 us
  local copies, waits for them, and re-layouts: 198 us -> 14.1 us
  blocking collectives: 124 us -> 0 us
  other arithmetic: 102 us -> 7.39 us
  starting transfers between devices: 41.3 us -> 0 us
    reduce_scatter x4 -> x0, waiting for transfers between devices: 451 us -> none  [the longest x1 173 us: side_by_side_2(): lax.psum_scatter(both, axis, scatter_dimension=dim, tiled=True)]
    all_gather x2 -> x0, waiting for transfers between devices: 353 us -> none  [the longest x1 187 us: gather_turned(): result, at, done = (lax.all_gather(both, axis, axis=0, tiled=True), 0, [])]
    pallas_call x0 -> x6, Pallas kernels: none -> 299 us  [the longest x1 76.3 us: attend_back(): pl.pallas_call(attend_back_kernel, out_shape=(jax.ShapeDtypeStruct((4, 2...]
    dot_general x105 -> x0, matrix products: 228 us -> none  [the longest x24 41.2 us: visit_block(): jnp.einsum('qgrd,kgd->grqk', query_heads, key_block, preferred_element_ty...]
    unnamed x8 -> x0, waiting for transfers between devices: 153 us -> none
    unnamed x1 -> x0, blocking collectives: 80.9 us -> none
    dynamic_slice x48 -> x1, local copies, waits for them, and re-layouts: 50.6 us -> 1.26 us  [on_device(): lax.dynamic_slice(terms, (D + own,), (32,))]
    all_to_all x10 -> x0, waiting for transfers between devices: 41.4 us -> none  [sent_to_all(): lax.all_to_all(jnp.broadcast_to(x[None], (peers, *x.shape)), axis, 0, 0,...]
  transfers between devices with their start and end apart: 17 -> 0, of which waited for: 15 -> 0; matrix products, arithmetic and copies ran while one was open for 6% -> 0% of each run, Pallas kernels for 0% -> 0%
where the time goes in v1:
time: 329 us; the launch traced here: 323 us
  Pallas kernels  299 us (91%)
  local copies, waits for them, and re-layouts  14.1 us (4%)
  other arithmetic  7.39 us (2%)
    pallas_call x1, Pallas kernels, attend_back(): pl.pallas_call(attend_back_kernel, out_shape=(jax.ShapeDtypeStruct((4, 2...  76.3 us
    pallas_call x1, Pallas kernels, attend(): pl.pallas_call(attend_kernel, out_shape=(jax.ShapeDtypeStruct((4, CH, 2 *...  74.5 us
    pallas_call x1, Pallas kernels, middle(): pl.pallas_call(middle_kernel, out_shape=(jax.ShapeDtypeStruct((2, HALF, D...  64.3 us
    pallas_call x1, Pallas kernels, finish(): pl.pallas_call(finish_kernel, out_shape=(jax.ShapeDtypeStruct((2, HALF, D...  44.3 us
    pallas_call x1, Pallas kernels, spread(): pl.pallas_call(spread_kernel, out_shape=(jax.ShapeDtypeStruct((4, 2, HALF...  34.1 us

profile of v1, /device:TPU:0, one launch (start us, length us, event | category | flops | bytes accessed | tf_op | source)
XLA Modules:
  0.0 322.8 jit_solution(5122802435188605084)
XLA Ops:
  0.6 0.0 copy-start
  0.7 0.7 compare_reduce_fusion
  1.4 1.3 select_reduce_fusion
  3.4 0.1 iota_add_fusion
  3.4 0.1 add.64
  3.5 0.7 subtract_convert_fusion
  4.2 0.0 copy-start.5
  4.2 0.0 copy-start.6
  4.2 0.0 copy-start.4
  4.2 1.4 fusion
  5.7 0.0 copy-start.7
  5.7 0.0 copy-start.9
  5.7 0.0 copy-start.8
  5.7 0.0 copy-start.10
  5.7 0.0 copy-start.11
  5.7 1.1 pad_maximum_fusion
  6.9 0.0 copy-done.5
  6.9 0.0 copy-start.12
  6.9 0.0 copy-start.13
  7.0 0.0 copy-done.7
  7.0 0.8 maximum_bitcast_fusion.w2
  7.8 0.0 copy-done.9
  7.8 0.7 maximum_bitcast_fusion.1.w1
  8.5 0.1 maximum_convert_fusion
  8.6 0.6 broadcast_in_dim.36.gains
  9.2 34.1 %spread.1 = (bf16[4,2,96,1024]{3,2,1,0:T(8,128)(2,1)}, bf16[4,2,96,1024]{3,2,1,0:T(8,128)(2,1)}, bf16[4,8,32,512]{3,2,1,0:T(8,128)(2,1)}, bf16[4,32,1408]{2,1,0:T(8,128)(2,1)}, f32[4,8,8,128]{3,2,1,0:T(8,128)}) custom-call(bf16[2,96,1024]{2,1,0:T(8,128)(2,1)} %bitcast.98, bf16[2,96,1024]{2,1,0:T(8,128)(2,1)} %bitcast.99, ...), custom_call_target="tpu_custom_call" | custom-call | tf_op jit(solution)/shard_map/spread/pallas_call | solution.py:248
  43.2 1.1 slice_reduce_fusion
  44.3 0.7 reshape_squeeze.6.gain
  45.0 0.5 bitcast_convert_fusion
  45.5 5.8 %make_heads.1 = (bf16[4,384,128]{2,1,0:T(8,128)(2,1)}, bf16[4,192,256]{2,1,0:T(8,128)(2,1)}, f32[768,384]{1,0:T(8,128)}, bf16[768,1024]{1,0:T(8,128)(2,1)}) custom-call(bf16[768,1024]{1,0:T(8,128)(2,1)} %bitcast.91, bf16[1024,512]{1,0:T(8,128)(2,1)} %bitcast.92, f32[1,1024]{1,0:T(1,128)} %reshape_squeeze.6.gain, f32[1,128]{1,0:T(1,128)} %get-tuple-element.86.qgain, ...), custom_call_target="tpu_custom_call" | custom-call | tf_op jit(solution)/shard_map/make_heads/pallas_call | solution.py:306
  51.3 74.5 %attend.1 = (bf16[4,192,256]{2,1,0:T(8,128)(2,1)}, f32[4,128,384]{2,1,0:T(8,128)}, f32[4,1,384]{2,1,0:T(1,128)}, bf16[4,8,192,256]{3,2,1,0:T(8,128)(2,1)}, bf16[4,8,32,1408]{3,2,1,0:T(8,128)(2,1)}) custom-call(bf16[4,384,128]{2,1,0:T(8,128)(2,1)} %get-tuple-element.42.q, bf16[4,192,256]{2,1,0:T(8,128)(2,1)} %get-tuple-element.43.kv, ...), custom_call_target="tpu_custom_call" | custom-call | tf_op jit(solution)/shard_map/attend/pallas_call | solution.py:440
  125.8 0.7 reshape_squeeze.7.gain
  126.5 64.3 %middle.1 = (bf16[2,96,1024]{2,1,0:T(8,128)(2,1)}, f32[96,1024]{1,0:T(8,128)}, bf16[4,384,128]{2,1,0:T(8,128)(2,1)}, bf16[1024,1408]{1,0:T(8,128)(2,1)}, f32[1,1024]{1,0:T(1,128)}) custom-call(bf16[4,192,256]{2,1,0:T(8,128)(2,1)} %get-tuple-element.45.att, bf16[1024,1408]{1,0:T(8,128)(2,1)} %bitcast.95, f32[1,1024]{1,0:T(1,128)} %reshape_squeeze.7.gain, ...), custom_call_target="tpu_custom_call" | custom-call | tf_op jit(solution)/shard_map/middle/pallas_call | solution.py:563
  190.8 76.3 %attend_back.1 = (f32[4,384,128]{2,1,0:T(8,128)}, f32[4,192,256]{2,1,0:T(8,128)}, bf16[4,32,1408]{2,1,0:T(8,128)(2,1)}) custom-call(bf16[4,384,128]{2,1,0:T(8,128)(2,1)} %get-tuple-element.42.q, bf16[4,8,192,256]{3,2,1,0:T(8,128)(2,1)} %get-tuple-element.49.kv_all, bf16[4,384,128]{2,1,0:T(8,128)(2,1)} %get-tuple-element.50.go, ...), custom_call_target="tpu_custom_call" | custom-call | tf_op jit(solution)/shard_map/attend_back/pallas_call | solution.py:682
  267.1 44.3 %finish.1 = (bf16[2,96,1024]{2,1,0:T(8,128)(2,1)}, f32[4,32,512]{2,1,0:T(8,128)}, f32[4,32,1408]{2,1,0:T(8,128)}, f32[24,128]{1,0:T(8,128)}) custom-call(f32[4,384,128]{2,1,0:T(8,128)} %get-tuple-element.54.dq, f32[4,192,256]{2,1,0:T(8,128)} %get-tuple-element.55.dkv, f32[768,384]{1,0:T(8,128)} %get-tuple-element.56.pre, ...), custom_call_target="tpu_custom_call" | custom-call | tf_op jit(solution)/shard_map/finish/pallas_call | solution.py:837
  311.5 1.2 slice_bitcast_fusion
  312.7 0.7 copy.55
  313.4 0.7 copy.53
  314.1 0.7 copy.54
  314.8 0.9 slice_bitcast_fusion.3
  315.7 0.7 copy.52
  316.3 0.7 copy.49
  317.0 0.6 copy.66
  317.7 0.6 copy.67
  318.3 1.3 fusion.1
  319.6 1.3 slice_bitcast_fusion.7
  320.8 0.7 copy.72
  321.6 0.7 copy.73
  (24 shorter events, 0.1 us)
Async XLA Ops:
  0.6 7.1 %copy-start = (bf16[32,512]{1,0:T(8,128)(2,1)S(1)}, bf16[32,512]{1,0:T(8,128)(2,1)}, u32[]{:S(2)}) copy-start(bf16[32,512]{1,0:T(8,128)(2,1)} %param.20) | copy-start | bytes 98308
  4.2 2.7 copy-start.5
  4.2 2.7 copy-start.6
  4.2 2.7 copy-start.4
  5.7 1.3 copy-start.7
  5.7 2.1 copy-start.9
  5.7 2.1 copy-start.8
  5.7 2.8 copy-start.10
  5.7 2.8 copy-start.11
  6.9 38.1 %copy-start.12 = (bf16[128]{0:T(256)(128)(2,1)S(1)}, bf16[128]{0:T(256)(128)(2,1)}, u32[]{:S(2)}) copy-start(bf16[128]{0:T(256)(128)(2,1)} %param.25) | copy-start | bytes 772
  6.9 38.1 %copy-start.13 = (bf16[128]{0:T(256)(128)(2,1)S(1)}, bf16[128]{0:T(256)(128)(2,1)}, u32[]{:S(2)}) copy-start(bf16[128]{0:T(256)(128)(2,1)} %param.24) | copy-start | bytes 772
  311.5 4.9 %copy-start.3 = (f32[4,32,512]{2,1,0:T(8,128)S(1)}, f32[4,32,512]{2,1,0:T(8,128)}, u32[]{:S(2)}) copy-start(f32[4,32,512]{2,1,0:T(8,128)} %get-tuple-element.62) | copy-start | bytes 786436
  312.7 8.2 %copy-start.1 = (bf16[2,96,1024]{2,1,0:T(8,128)(2,1)S(1)}, bf16[2,96,1024]{2,1,0:T(8,128)(2,1)}, u32[]{:S(2)}) copy-start(bf16[2,96,1024]{2,1,0:T(8,128)(2,1)} %get-tuple-element.48) | copy-start | bytes 1179652
  313.4 8.2 %copy-start.2 = (bf16[2,96,1024]{2,1,0:T(8,128)(2,1)S(1)}, bf16[2,96,1024]{2,1,0:T(8,128)(2,1)}, u32[]{:S(2)}) copy-start(bf16[2,96,1024]{2,1,0:T(8,128)(2,1)} %get-tuple-element.61) | copy-start | bytes 1179652
